TPU v7x, 32 devices: a whole 2x2x4 slice. The times are simulated.
32 devices in a mesh: ctx: 8 (over z, y), uly: 4 (over x, core).
Axes of the slice: x: 2, y: 2, z: 4, core: 2. Of those that a mesh axis runs over, the one named last changes fastest.
Arguments:
- queries: bfloat16 [8192, 4096], P(('ctx', 'uly')), may hold values from -12 to 12
- key_rows: bfloat16 [8192, 2048], P(('ctx', 'uly')), may hold values from -12 to 12
- value_rows: bfloat16 [8192, 2048], P(('ctx', 'uly')), may hold values from -6 to 6
- doc_lengths: int32 [8], replicated, may hold values from 1 to 2048, 8192 in all
Outputs:
- attended: bfloat16 [8192, 4096], P(('ctx', 'uly'))
Inputs may be any that keep to these rules, and one draw needn't show every extreme that they name: `doc_lengths`: the 8 documents are packed in order and their lengths sum to 8192; the longest is exactly 2048.
All inputs are finite; a program needn't handle non-finite values.
Results may differ from a plain program's by a relative error of at most 0.005.
Values may be sent and summed in bfloat16 or wider, within the bound.
A program may use at most 64 MiB of HBM per device.

v0:
```python
from functools import partial

import jax
import jax.numpy as jnp
from jax import lax
from jax.sharding import PartitionSpec as P

HD = 128
SPAN = 2


query_scale = 144.0 ** (-0.5)
logit_cap = 50.0


def from_behind(block, axis, distance):
    devices = range(lax.axis_size(axis))
    route = [(i - distance, i) for i in devices if i - distance in devices]
    return lax.ppermute(block, axis, route)


def doc_index(doc_lengths, positions):
    doc_ends = jnp.cumsum(doc_lengths, dtype=jnp.int32)
    return jnp.sum(
        (doc_ends[None, :] <= positions[:, None]).astype(jnp.int32), axis=1, dtype=jnp.int32
    )


def key_piece(key_block, value_block, doc_lengths, first_pos):
    positions = first_pos + jnp.arange(key_block.shape[0], dtype=jnp.int32)
    key_doc = doc_index(doc_lengths, jnp.maximum(positions, 0))
    return (key_block, value_block, positions, key_doc)


def add_piece(key_head, value_head, key_pos, key_doc, stacked, query_pos, query_doc, state_pair):
    numerator, row_total = state_pair
    scores = lax.dot_general(
        stacked, key_head, (((1,), (1,)), ((), ())), preferred_element_type=jnp.float32
    )
    capped = logit_cap * jnp.tanh(scores * query_scale / logit_cap)
    allowed = (
        (key_doc[None, :] == query_doc[:, None])
        & (key_pos[None, :] <= query_pos[:, None])
        & (key_pos[None, :] >= 0)
    )
    weights = jnp.where(allowed, jnp.exp(capped), 0.0)
    row_total = row_total + jnp.sum(weights, axis=1)
    numerator = numerator + jnp.dot(
        weights.astype(jnp.bfloat16), value_head, preferred_element_type=jnp.float32
    )
    return (numerator, row_total)


def head_block(queries, pieces, query_pos, query_doc, head_index):
    query_len = queries.shape[0]
    head_pair = lax.dynamic_slice_in_dim(queries, head_index * 2 * HD, 2 * HD, 1)
    stacked = jnp.concatenate([head_pair[:, :HD], head_pair[:, HD:]], axis=0)
    doubled_pos = jnp.concatenate([query_pos, query_pos])
    doubled_doc = jnp.concatenate([query_doc, query_doc])
    state_pair = (
        jnp.zeros((2 * query_len, HD), jnp.float32),
        jnp.zeros((2 * query_len,), jnp.float32),
    )
    for key_block, value_block, key_pos, key_doc, is_live in pieces:
        key_head = lax.dynamic_slice_in_dim(key_block, head_index * HD, HD, 1)
        value_head = lax.dynamic_slice_in_dim(value_block, head_index * HD, HD, 1)
        update = partial(
            add_piece, key_head, value_head, key_pos, key_doc, stacked, doubled_pos, doubled_doc
        )
        state_pair = update(state_pair)
    numerator, row_total = state_pair
    result = numerator / row_total[:, None]
    return jnp.concatenate([result[:query_len], result[query_len:]], axis=1)


def attend(queries, pieces, first_pos, doc_lengths):
    query_len = queries.shape[0]
    query_pos = first_pos + jnp.arange(query_len, dtype=jnp.int32)
    query_doc = doc_index(doc_lengths, query_pos)
    marked = []
    for key_block, value_block, key_pos, key_doc in pieces:
        is_live = (key_pos[0] >= 0) & (key_doc[-1] >= query_doc[0])
        marked.append((key_block, value_block, key_pos, key_doc, is_live))
    head_count = queries.shape[1] // (2 * HD)
    per_head = lax.map(
        partial(head_block, queries, marked, query_pos, query_doc),
        jnp.arange(head_count, dtype=jnp.int32),
    )
    return (
        jnp.transpose(per_head, (1, 0, 2))
        .reshape(query_len, head_count * 2 * HD)
        .astype(jnp.bfloat16)
    )


def shards(queries, key_rows, value_rows, doc_lengths):
    shard_len = queries.shape[0]
    first_pos = (lax.axis_index("ctx") * lax.axis_size("uly") + lax.axis_index("uly")) * shard_len
    pieces = [key_piece(key_rows, value_rows, doc_lengths, first_pos)]
    for offset in range(1, SPAN * lax.axis_size("uly") + 1):
        moved_keys, moved_values = from_behind((key_rows, value_rows), ("ctx", "uly"), offset)
        pieces.append(
            key_piece(moved_keys, moved_values, doc_lengths, first_pos - offset * shard_len)
        )
    return attend(queries, pieces, first_pos, doc_lengths)


def solution(mesh):
    placed = (P(("ctx", "uly"), None), P(("ctx", "uly"), None), P(("ctx", "uly"), None), P())
    return jax.shard_map(
        shards, mesh=mesh, in_specs=placed, out_specs=P(("ctx", "uly"), None), check_vma=False
    )
```

profile of v0, /device:TPU:31, one launch (start us, length us, event | category | flops | bytes accessed | tf_op | source)
XLA Modules:
  0.0 838.4 jit_solution(2907940624437751022)
XLA Ops:
  0.0 1.3 collective-permute-start
  1.3 1.3 collective-permute-start.1
  2.6 1.3 collective-permute-start.2
  3.9 1.3 collective-permute-start.3
  5.2 1.3 collective-permute-start.4
  6.5 1.3 collective-permute-start.5
  7.8 1.3 collective-permute-start.6
  9.1 59.1 %collective-permute-done.2 = bf16[256,2048]{1,0:T(8,128)(2,1)} collective-permute-done((bf16[256,2048]{1,0:T(8,128)(2,1)}, bf16[256,2048]{1,0:T(8,128)(2,1)}, u32[]{:S(2)}, u32[]{:S(2)}) %collective-permute-start.2) | collective-permute-done | bytes 1048608 | tf_op jit(solution)/shard_map/ppermute | solution.py:19
  68.2 1.3 collective-permute-start.7
  69.5 20.9 %collective-permute-done.3 = bf16[256,2048]{1,0:T(8,128)(2,1)S(1)} collective-permute-done((bf16[256,2048]{1,0:T(8,128)(2,1)}, bf16[256,2048]{1,0:T(8,128)(2,1)S(1)}, u32[]{:S(2)}, u32[]{:S(2)}) %collective-permute-start.3) | collective-permute-done | bytes 1048608 | tf_op jit(solution)/shard_map/ppermute | solution.py:19
  90.3 1.3 collective-permute-start.8
  91.6 1.3 collective-permute-start.9
  92.9 2.0 collective-permute-done.5
  95.0 1.3 collective-permute-start.10
  96.3 1.3 collective-permute-start.11
  97.6 1.3 collective-permute-start.12
  98.9 19.0 %collective-permute-done.8 = bf16[256,2048]{1,0:T(8,128)(2,1)S(1)} collective-permute-done((bf16[256,2048]{1,0:T(8,128)(2,1)}, bf16[256,2048]{1,0:T(8,128)(2,1)S(1)}, u32[]{:S(2)}, u32[]{:S(2)}) %collective-permute-start.8) | collective-permute-done | bytes 1048608 | tf_op jit(solution)/shard_map/ppermute | solution.py:19
  117.9 1.3 collective-permute-start.13
  119.2 111.9 %collective-permute-done.9 = bf16[256,2048]{1,0:T(8,128)(2,1)S(1)} collective-permute-done((bf16[256,2048]{1,0:T(8,128)(2,1)}, bf16[256,2048]{1,0:T(8,128)(2,1)S(1)}, u32[]{:S(2)}, u32[]{:S(2)}) %collective-permute-start.9) | collective-permute-done | bytes 1048608 | tf_op jit(solution)/shard_map/ppermute | solution.py:19
  231.1 1.3 collective-permute-start.14
  233.5 1.3 collective-permute-start.15
  235.9 219.3 %collective-permute-done.14 = bf16[256,2048]{1,0:T(8,128)(2,1)} collective-permute-done((bf16[256,2048]{1,0:T(8,128)(2,1)}, bf16[256,2048]{1,0:T(8,128)(2,1)}, u32[]{:S(2)}, u32[]{:S(2)}) %collective-permute-start.14) | collective-permute-done | bytes 1048608 | tf_op jit(solution)/shard_map/ppermute | solution.py:19
  455.2 11.2 %collective-permute-done.15 = bf16[256,2048]{1,0:T(8,128)(2,1)} collective-permute-done((bf16[256,2048]{1,0:T(8,128)(2,1)}, bf16[256,2048]{1,0:T(8,128)(2,1)}, u32[]{:S(2)}, u32[]{:S(2)}) %collective-permute-start.15) | collective-permute-done | bytes 1048608 | tf_op jit(solution)/shard_map/ppermute | solution.py:19
  466.4 369.1 %while.15 = (s32[]{:T(128)}, bf16[16,256,256]{1,2,0:T(8,128)(2,1)S(1)}, s32[256]{0:T(256)S(1)}, s32[512]{0:T(512)S(1)}, s32[512]{0:T(512)S(1)}, /*index=5*/s32[1...) while((s32[]{:T(128)}, ...), condition=%wide.region_21.22_spmd.clone, body=%wide.region_11.21_spmd.clone.sunk | while | flops 617879808 | bytes 12300469 | solution.py:85
  471.7 1.2 fusion.172
  517.9 1.2 fusion.172
  540.9 1.2 fusion.172
  587.1 1.2 fusion.172
  656.3 1.2 fusion.172
  771.6 1.2 fusion.172
  800.8 1.2 fusion.175
  835.5 2.9 copy.7
  (556 shorter events, 337.0 us)
Async XLA Ops:
  0.0 6.5 collective-permute-start
  1.3 6.5 collective-permute-start.1
  2.6 65.6 %collective-permute-start.2 = (bf16[256,2048]{1,0:T(8,128)(2,1)}, bf16[256,2048]{1,0:T(8,128)(2,1)}, u32[]{:S(2)}, u32[]{:S(2)}) collective-permute-start(bf16[256,2048]{1,0:T(8,128)(2,1)} %param.7), channel_id=1, source_target_pairs={{0,2},{1,3},{2,4},{3,5},{4,6},{5,7},{6,8},{7,9},{8,10},{9,11},{10,... | collective-permute-start | bytes 3145736 | tf_op jit(solution)/shard_map/ppermute | solution.py:19
  3.9 86.5 %collective-permute-start.3 = (bf16[256,2048]{1,0:T(8,128)(2,1)}, bf16[256,2048]{1,0:T(8,128)(2,1)S(1)}, u32[]{:S(2)}, u32[]{:S(2)}) collective-permute-start(bf16[256,2048]{1,0:T(8,128)(2,1)} %param.8), channel_id=1, source_target_pairs={{0,2},{1,3},{2,4},{3,5},{4,6},{5,7},{6,8},{7,9},{8,10},{9,11},{10,... | collective-permute-start | bytes 3145736 | tf_op jit(solution)/shard_map/ppermute | solution.py:19
  5.2 86.5 %collective-permute-start.4 = (bf16[256,2048]{1,0:T(8,128)(2,1)}, bf16[256,2048]{1,0:T(8,128)(2,1)}, u32[]{:S(2)}, u32[]{:S(2)}) collective-permute-start(bf16[256,2048]{1,0:T(8,128)(2,1)} %param.7), channel_id=1, source_target_pairs={{0,3},{1,4},{2,5},{3,6},{4,7},{5,8},{6,9},{7,10},{8,11},{9,12},{10... | collective-permute-start | bytes 3145736 | tf_op jit(solution)/shard_map/ppermute | solution.py:19
  6.5 88.5 %collective-permute-start.5 = (bf16[256,2048]{1,0:T(8,128)(2,1)}, bf16[256,2048]{1,0:T(8,128)(2,1)S(1)}, u32[]{:S(2)}, u32[]{:S(2)}) collective-permute-start(bf16[256,2048]{1,0:T(8,128)(2,1)} %param.8), channel_id=1, source_target_pairs={{0,3},{1,4},{2,5},{3,6},{4,7},{5,8},{6,9},{7,10},{8,11},{9,12},{10... | collective-permute-start | bytes 3145736 | tf_op jit(solution)/shard_map/ppermute | solution.py:19
  7.8 88.4 %collective-permute-start.6 = (bf16[256,2048]{1,0:T(8,128)(2,1)}, bf16[256,2048]{1,0:T(8,128)(2,1)S(1)}, u32[]{:S(2)}, u32[]{:S(2)}) collective-permute-start(bf16[256,2048]{1,0:T(8,128)(2,1)} %param.7), channel_id=1, source_target_pairs={{0,4},{1,5},{2,6},{3,7},{4,8},{5,9},{6,10},{7,11},{8,12},{9,13},{1... | collective-permute-start | bytes 3145736 | tf_op jit(solution)/shard_map/ppermute | solution.py:19
  68.2 29.4 %collective-permute-start.7 = (bf16[256,2048]{1,0:T(8,128)(2,1)}, bf16[256,2048]{1,0:T(8,128)(2,1)S(1)}, u32[]{:S(2)}, u32[]{:S(2)}) collective-permute-start(bf16[256,2048]{1,0:T(8,128)(2,1)} %param.8), channel_id=1, source_target_pairs={{0,4},{1,5},{2,6},{3,7},{4,8},{5,9},{6,10},{7,11},{8,12},{9,13},{1... | collective-permute-start | bytes 3145736 | tf_op jit(solution)/shard_map/ppermute | solution.py:19
  90.3 142.0 %copy-start = (bf16[256,2048]{1,0:T(8,128)(2,1)}, bf16[256,2048]{1,0:T(8,128)(2,1)S(1)}, u32[]{:S(2)}) copy-start(bf16[256,2048]{1,0:T(8,128)(2,1)S(1)} %collective-permute-done.3) | copy-start | bytes 3145732
  90.3 27.6 %collective-permute-start.8 = (bf16[256,2048]{1,0:T(8,128)(2,1)}, bf16[256,2048]{1,0:T(8,128)(2,1)S(1)}, u32[]{:S(2)}, u32[]{:S(2)}) collective-permute-start(bf16[256,2048]{1,0:T(8,128)(2,1)} %param.7), channel_id=1, source_target_pairs={{0,5},{1,6},{2,7},{3,8},{4,9},{5,10},{6,11},{7,12},{8,13},{9,14},{... | collective-permute-start | bytes 3145736 | tf_op jit(solution)/shard_map/ppermute | solution.py:19
  91.6 139.4 %collective-permute-start.9 = (bf16[256,2048]{1,0:T(8,128)(2,1)}, bf16[256,2048]{1,0:T(8,128)(2,1)S(1)}, u32[]{:S(2)}, u32[]{:S(2)}) collective-permute-start(bf16[256,2048]{1,0:T(8,128)(2,1)} %param.8), channel_id=1, source_target_pairs={{0,5},{1,6},{2,7},{3,8},{4,9},{5,10},{6,11},{7,12},{8,13},{9,14},{... | collective-permute-start | bytes 3145736 | tf_op jit(solution)/shard_map/ppermute | solution.py:19
  95.0 137.4 %copy-start.1 = (bf16[256,2048]{1,0:T(8,128)(2,1)}, bf16[256,2048]{1,0:T(8,128)(2,1)S(1)}, u32[]{:S(2)}) copy-start(bf16[256,2048]{1,0:T(8,128)(2,1)S(1)} %collective-permute-done.5) | copy-start | bytes 3145732
  95.0 137.4 %collective-permute-start.10 = (bf16[256,2048]{1,0:T(8,128)(2,1)}, bf16[256,2048]{1,0:T(8,128)(2,1)S(1)}, u32[]{:S(2)}, u32[]{:S(2)}) collective-permute-start(bf16[256,2048]{1,0:T(8,128)(2,1)} %param.7), channel_id=1, source_target_pairs={{0,6},{1,7},{2,8},{3,9},{4,10},{5,11},{6,12},{7,13},{8,14},{9,15},... | collective-permute-start | bytes 3145736 | tf_op jit(solution)/shard_map/ppermute | solution.py:19
  96.3 136.1 %copy-start.4 = (bf16[256,2048]{1,0:T(8,128)(2,1)}, bf16[256,2048]{1,0:T(8,128)(2,1)S(1)}, u32[]{:S(2)}) copy-start(bf16[256,2048]{1,0:T(8,128)(2,1)S(1)} %collective-permute-done.6) | copy-start | bytes 3145732
  96.3 139.6 %collective-permute-start.11 = (bf16[256,2048]{1,0:T(8,128)(2,1)}, bf16[256,2048]{1,0:T(8,128)(2,1)}, u32[]{:S(2)}, u32[]{:S(2)}) collective-permute-start(bf16[256,2048]{1,0:T(8,128)(2,1)} %param.8), channel_id=1, source_target_pairs={{0,6},{1,7},{2,8},{3,9},{4,10},{5,11},{6,12},{7,13},{8,14},{9,15},... | collective-permute-start | bytes 3145736 | tf_op jit(solution)/shard_map/ppermute | solution.py:19
  97.6 134.8 %copy-start.2 = (bf16[256,2048]{1,0:T(8,128)(2,1)}, bf16[256,2048]{1,0:T(8,128)(2,1)S(1)}, u32[]{:S(2)}) copy-start(bf16[256,2048]{1,0:T(8,128)(2,1)S(1)} %collective-permute-done.7) | copy-start | bytes 3145732
  97.6 138.3 %collective-permute-start.12 = (bf16[256,2048]{1,0:T(8,128)(2,1)}, bf16[256,2048]{1,0:T(8,128)(2,1)}, u32[]{:S(2)}, u32[]{:S(2)}) collective-permute-start(bf16[256,2048]{1,0:T(8,128)(2,1)} %param.7), channel_id=1, source_target_pairs={{0,7},{1,8},{2,9},{3,10},{4,11},{5,12},{6,13},{7,14},{8,15},{9,16}... | collective-permute-start | bytes 3145736 | tf_op jit(solution)/shard_map/ppermute | solution.py:19
  117.9 114.5 %copy-start.5 = (bf16[256,2048]{1,0:T(8,128)(2,1)}, bf16[256,2048]{1,0:T(8,128)(2,1)S(1)}, u32[]{:S(2)}) copy-start(bf16[256,2048]{1,0:T(8,128)(2,1)S(1)} %collective-permute-done.8) | copy-start | bytes 3145732
  117.9 118.0 %collective-permute-start.13 = (bf16[256,2048]{1,0:T(8,128)(2,1)}, bf16[256,2048]{1,0:T(8,128)(2,1)}, u32[]{:S(2)}, u32[]{:S(2)}) collective-permute-start(bf16[256,2048]{1,0:T(8,128)(2,1)} %param.8), channel_id=1, source_target_pairs={{0,7},{1,8},{2,9},{3,10},{4,11},{5,12},{6,13},{7,14},{8,15},{9,16}... | collective-permute-start | bytes 3145736 | tf_op jit(solution)/shard_map/ppermute | solution.py:19
  231.1 1.4 copy-start.3
  231.1 224.1 %collective-permute-start.14 = (bf16[256,2048]{1,0:T(8,128)(2,1)}, bf16[256,2048]{1,0:T(8,128)(2,1)}, u32[]{:S(2)}, u32[]{:S(2)}) collective-permute-start(bf16[256,2048]{1,0:T(8,128)(2,1)} %param.7), channel_id=1, source_target_pairs={{0,8},{1,9},{2,10},{3,11},{4,12},{5,13},{6,14},{7,15},{8,16},{9,17... | collective-permute-start | bytes 3145736 | tf_op jit(solution)/shard_map/ppermute | solution.py:19
  232.4 1.1 copy-start.6
  233.5 232.9 %collective-permute-start.15 = (bf16[256,2048]{1,0:T(8,128)(2,1)}, bf16[256,2048]{1,0:T(8,128)(2,1)}, u32[]{:S(2)}, u32[]{:S(2)}) collective-permute-start(bf16[256,2048]{1,0:T(8,128)(2,1)} %param.8), channel_id=1, source_target_pairs={{0,8},{1,9},{2,10},{3,11},{4,12},{5,13},{6,14},{7,15},{8,16},{9,17... | collective-permute-start | bytes 3145736 | tf_op jit(solution)/shard_map/ppermute | solution.py:19
where the time goes:
time: 853 us; the launch traced here: 838 us
  waiting for transfers between devices  443 us (52%)
  matrix products  317 us (37%)
  local copies, waits for them, and re-layouts  29 us (3%)
  loops' own time  25.7 us (3%)
  starting transfers between devices  20.6 us (2%)
    ppermute x16, waiting for transfers between devices, from_behind(): return lax.ppermute(block, axis, route)  443 us
    dot_general x144, matrix products, add_piece(): lax.dot_general(stacked, key_head, (((1,), (1,)), ((), ())), preferred_el...  175 us
    dot_general x144, matrix products, add_piece(): jnp.dot(weights.astype(jnp.bfloat16), value_head, preferred_element_type=...  142 us
    another operation x1, loops' own time, attend(): lax.map(partial(head_block, queries, marked, query_pos, query_doc), jnp.a...  25.7 us
    ppermute x16, starting transfers between devices, from_behind(): return lax.ppermute(block, axis, route)  20.6 us
  transfers between devices with their start and end apart: 16, of which 7 were waited for; matrix products, arithmetic and copies ran while one was open for 0% of the time, Pallas kernels for 0%

commit v1 on v0

v1 whole, which is shorter than its diff:
```python
import functools
import math

import jax
import jax.numpy as jnp
from jax import lax
from jax.experimental import pallas as pl
from jax.experimental.pallas import tpu as pltpu
from jax.sharding import PartitionSpec as P

HD = 128
SPAN = 2
MESH = pl.DeviceIdType.MESH
SCALE = 144.0 ** (-0.5) / 50.0
CAP = 50.0 * math.log2(math.e)


def kernel(
    n_ctx, n_uly, lens_ref, q_ref, k_ref, v_ref, out_ref,
    q_all, k_all, v_all, out_buf, starts, acc, total,
    own_sem, kv_send, kv_recv, q_send, q_recv, halo_send, halo_recv, out_send, out_recv,
):
    size = SPAN * n_uly
    groups = n_ctx // SPAN
    rows = q_ref.shape[0]
    kv_cols = k_ref.shape[1] // size
    q_cols = q_ref.shape[1] // size
    kv_heads = kv_cols // HD
    share = q_cols // kv_cols
    me = lax.axis_index("ctx") * n_uly + lax.axis_index("uly")
    group, rank = me // size, me % size
    has_next = group < groups - 1
    has_prev = group > 0

    def device(g, r):
        flat = g * size + r
        return (flat // n_uly, flat % n_uly)

    def cols(r, width):
        return pl.ds(pl.multiple_of(r * width, width), width)

    barrier = pltpu.get_barrier_semaphore()
    for d in range(1, size):
        pl.semaphore_signal(barrier, inc=1, device_id=device(group, (rank + d) % size), device_id_type=MESH)

    @pl.when(has_next)
    def _():
        pl.semaphore_signal(barrier, inc=1, device_id=device(group + 1, rank), device_id_type=MESH)

    @pl.when(has_prev)
    def _():
        pl.semaphore_signal(barrier, inc=1, device_id=device(group - 1, rank), device_id_type=MESH)

    pl.semaphore_wait(barrier, size - 1 + jnp.where(has_next, 1, 0) + jnp.where(has_prev, 1, 0))

    def kv_copy(d):
        peer = (rank + d) % size
        return [
            pltpu.make_async_remote_copy(
                src_ref=src.at[:, cols(peer, kv_cols)],
                dst_ref=dst.at[size + rank],
                send_sem=kv_send.at[n, peer],
                recv_sem=kv_recv.at[n, rank],
                device_id=device(group, peer),
                device_id_type=MESH,
            )
            for n, (src, dst) in enumerate(((k_ref, k_all), (v_ref, v_all)))
        ]

    def q_copy(peer):
        return pltpu.make_async_remote_copy(
            src_ref=q_ref.at[:, cols(peer, q_cols)],
            dst_ref=q_all.at[rank],
            send_sem=q_send.at[peer],
            recv_sem=q_recv.at[rank],
            device_id=device(group, peer),
            device_id_type=MESH,
        )

    def halo_copy(s):
        return [
            pltpu.make_async_remote_copy(
                src_ref=buf.at[size + s],
                dst_ref=buf.at[s],
                send_sem=halo_send.at[n, s],
                recv_sem=halo_recv.at[n, s],
                device_id=device(group + 1, rank),
                device_id_type=MESH,
            )
            for n, buf in enumerate((k_all, v_all))
        ]

    def out_copy(i):
        return pltpu.make_async_remote_copy(
            src_ref=out_buf.at[i],
            dst_ref=out_ref.at[:, cols(rank, q_cols)],
            send_sem=out_send.at[i],
            recv_sem=out_recv.at[rank],
            device_id=device(group, i),
            device_id_type=MESH,
        )

    def arrived(dst, sem):
        pltpu.make_async_copy(dst, dst, sem).wait()

    for d in range(1, size):
        for copy in kv_copy(d):
            copy.start()
    own = [
        pltpu.make_async_copy(k_ref.at[:, cols(rank, kv_cols)], k_all.at[size + rank], own_sem.at[0]),
        pltpu.make_async_copy(v_ref.at[:, cols(rank, kv_cols)], v_all.at[size + rank], own_sem.at[1]),
        pltpu.make_async_copy(q_ref.at[:, cols(rank, q_cols)], q_all.at[rank], own_sem.at[2]),
    ]
    for copy in own:
        copy.start()

    origin = (group - 1) * size * rows

    def find_starts(i, _):
        positions = group * size * rows + i * rows + lax.broadcasted_iota(jnp.int32, (rows, HD), 0)

        def next_doc(n, carry):
            begin, found = carry
            return begin + lens_ref[n], jnp.where(begin <= positions, begin, found)

        _, found = lax.fori_loop(
            0, lens_ref.shape[0], next_doc, (jnp.int32(0), jnp.zeros((rows, HD), jnp.int32))
        )
        starts[i] = found - origin
        return 0

    lax.fori_loop(0, size, find_starts, 0)

    for copy in own:
        copy.wait()
    for d in range(size):
        source = (rank + size - d) % size
        if d:
            for n, buf in enumerate((k_all, v_all)):
                arrived(buf.at[size + source], kv_recv.at[n, source])

        @pl.when(has_next)
        def _():
            for copy in halo_copy(source):
                copy.start()

        if d:
            q_copy((rank + d) % size).start()

    def block(i, slot, causal, first):
        begin = starts[i] - slot * rows
        begin = jnp.concatenate([begin] * (rows // HD), axis=1)
        place = lax.broadcasted_iota(jnp.int32, (rows, rows), 1)
        allowed = place >= begin
        if causal:
            allowed = allowed & (place <= lax.broadcasted_iota(jnp.int32, (rows, rows), 0))
        for h in range(kv_heads):
            key = k_all[slot, :, h * HD:(h + 1) * HD]
            value = v_all[slot, :, h * HD:(h + 1) * HD]
            for j in range(h * share, (h + 1) * share):
                query = q_all[i, :, j * HD:(j + 1) * HD]
                scores = lax.dot_general(
                    query, key, (((1,), (1,)), ((), ())), preferred_element_type=jnp.float32
                )
                weights = jnp.where(allowed, jnp.exp2(jnp.tanh(scores * SCALE) * CAP), 0.0)
                part = sum(weights[:, c * HD:(c + 1) * HD] for c in range(rows // HD))
                product = jnp.dot(
                    weights.astype(jnp.bfloat16), value, preferred_element_type=jnp.float32
                )
                if first:
                    total[i, j] = part
                    acc[i, j] = product
                else:
                    total[i, j] += part
                    acc[i, j] += product

    def own_part(i, _):
        @pl.when(i != rank)
        def _():
            arrived(q_all.at[i], q_recv.at[i])

        block(i, size + i, True, True)

        def step(j, _):
            block(i, size + j, False, False)
            return 0

        lax.fori_loop(0, i, step, 0)
        return 0

    lax.fori_loop(0, size, own_part, 0)

    def halo_part(n, _):
        i = size - 1 - n

        @pl.when(has_prev)
        def _():
            for m, buf in enumerate((k_all, v_all)):
                arrived(buf.at[i], halo_recv.at[m, i])

        def step(j, _):
            block(i, j, False, False)
            return 0

        lax.fori_loop(i, jnp.where(has_prev, size, 0), step, 0)
        for j in range(kv_heads * share):
            row_total = jnp.sum(total[i, j], axis=1, keepdims=True)
            out_buf[i, :, j * HD:(j + 1) * HD] = (acc[i, j] / row_total).astype(jnp.bfloat16)

        @pl.when(i != rank)
        def _():
            out_copy(i).start()

        @pl.when(i == rank)
        def _():
            pltpu.make_async_copy(out_buf.at[i], out_ref.at[:, cols(rank, q_cols)], own_sem.at[0]).start()

        return 0

    lax.fori_loop(0, size, halo_part, 0)

    pltpu.make_async_copy(out_buf.at[rank], out_ref.at[:, cols(rank, q_cols)], own_sem.at[0]).wait()
    for d in range(1, size):
        peer = (rank + d) % size
        for copy in kv_copy(d):
            copy.wait_send()
        q_copy(peer).wait_send()
        out_copy(peer).wait_send()
        arrived(out_ref.at[:, cols(peer, q_cols)], out_recv.at[peer])

    @pl.when(has_next)
    def _():
        for s in range(size):
            for copy in halo_copy(s):
                copy.wait_send()


def shards(n_ctx, n_uly, queries, key_rows, value_rows, doc_lengths):
    size = SPAN * n_uly
    rows, q_width = queries.shape
    kv_cols, q_cols = key_rows.shape[1] // size, q_width // size
    heads = q_cols // HD
    dma = pltpu.SemaphoreType.DMA
    return pl.pallas_call(
        functools.partial(kernel, n_ctx, n_uly),
        out_shape=jax.ShapeDtypeStruct(queries.shape, jnp.bfloat16),
        in_specs=[pl.BlockSpec(memory_space=pltpu.SMEM)] + [pl.BlockSpec(memory_space=pl.ANY)] * 3,
        out_specs=pl.BlockSpec(memory_space=pl.ANY),
        scratch_shapes=[
            pltpu.VMEM((size, rows, q_cols), jnp.bfloat16),
            pltpu.VMEM((2 * size, rows, kv_cols), jnp.bfloat16),
            pltpu.VMEM((2 * size, rows, kv_cols), jnp.bfloat16),
            pltpu.VMEM((size, rows, q_cols), jnp.bfloat16),
            pltpu.VMEM((size, rows, HD), jnp.int32),
            pltpu.VMEM((size, heads, rows, HD), jnp.float32),
            pltpu.VMEM((size, heads, rows, HD), jnp.float32),
            dma((3,)),
            dma((2, size)),
            dma((2, size)),
            dma((size,)),
            dma((size,)),
            dma((2, size)),
            dma((2, size)),
            dma((size,)),
            dma((size,)),
        ],
        compiler_params=pltpu.CompilerParams(
            collective_id=0, has_side_effects=True, vmem_limit_bytes=48 * 1024 * 1024
        ),
    )(doc_lengths, queries, key_rows, value_rows)


def solution(mesh):
    placed = (P(("ctx", "uly"), None), P(("ctx", "uly"), None), P(("ctx", "uly"), None), P())
    return jax.shard_map(
        functools.partial(shards, mesh.shape["ctx"], mesh.shape["uly"]),
        mesh=mesh, in_specs=placed, out_specs=P(("ctx", "uly"), None), check_vma=False,
    )
```

time: 853 us -> 123 us (0.14)
  the two profiles are of different devices: /device:TPU:31 before, /device:TPU:8 now
where the time goes in v1:
time: 123 us; the launch traced here: 122 us
  Pallas kernels  118 us (96%)
  local copies, waits for them, and re-layouts  4.42 us (4%)
    pallas_call x1, Pallas kernels, shards(): pl.pallas_call(functools.partial(kernel, n_ctx, n_uly), out_shape=jax.Sha...  118 us
    unnamed x7, local copies, waits for them, and re-layouts  4.42 us

profile of v1, /device:TPU:8, one launch (start us, length us, event | category | flops | bytes accessed | tf_op | source)
XLA Modules:
  0.0 122.3 jit_solution(3322525339293182398)
XLA Ops:
  0.0 0.0 copy-start
  0.0 1.2 copy-done
  1.2 0.0 copy-start.1
  1.2 1.2 copy-done.1
  2.5 0.0 copy-start.2
  2.5 0.7 copy-done.2
  3.1 117.9 %shard_map.46 = bf16[256,4096]{1,0:T(8,128)(2,1)S(1)} custom-call(s32[8]{0:T(128)S(1)} %copy-done.2, bf16[256,4096]{1,0:T(8,128)(2,1)} %q_ref.1, bf16[256,2048]{1,0:T(8,128)(2,1)S(1)} %copy-done, bf16[256,2048]{1,0:T(8,128)(2,1)S(1)} %copy-done.1), custom_call_target="tpu_custom_call" | custom-call | tf_op jit(solution)/shard_map/pallas_call | solution.py:244
  121.0 1.3 %copy.6 = bf16[256,4096]{1,0:T(8,128)(2,1)} copy(bf16[256,4096]{1,0:T(8,128)(2,1)S(1)} %shard_map.46) | data formatting | bytes 4194304
Async XLA Ops:
  0.0 1.2 %copy-start = (bf16[256,2048]{1,0:T(8,128)(2,1)S(1)}, bf16[256,2048]{1,0:T(8,128)(2,1)}, u32[]{:S(2)}) copy-start(bf16[256,2048]{1,0:T(8,128)(2,1)} %k_ref.1) | copy-start | bytes 3145732
  1.2 1.2 %copy-start.1 = (bf16[256,2048]{1,0:T(8,128)(2,1)S(1)}, bf16[256,2048]{1,0:T(8,128)(2,1)}, u32[]{:S(2)}) copy-start(bf16[256,2048]{1,0:T(8,128)(2,1)} %v_ref.1) | copy-start | bytes 3145732
  2.5 0.7 copy-start.2

commit v2 on v1

v2 whole, which is shorter than its diff:
```python
import functools
import math

import jax
import jax.numpy as jnp
from jax import lax
from jax.experimental import pallas as pl
from jax.experimental.pallas import tpu as pltpu
from jax.sharding import PartitionSpec as P

HD = 128
SPAN = 2
MESH = pl.DeviceIdType.MESH
SCALE = 144.0 ** (-0.5) / 50.0
CAP = 50.0 * math.log2(math.e)


def kernel(
    n_ctx, n_uly, lens_ref, q_ref, k_ref, v_ref, out_ref,
    q_all, k_all, v_all, out_buf, starts, acc, total,
    own_sem, kv_send, kv_recv, q_send, q_recv, halo_send, halo_recv, out_send, out_recv,
):
    size = SPAN * n_uly
    groups = n_ctx // SPAN
    rows = q_ref.shape[0]
    kv_cols = k_ref.shape[1] // size
    q_cols = q_ref.shape[1] // size
    kv_heads = kv_cols // HD
    share = q_cols // kv_cols
    width = share * HD
    me = lax.axis_index("ctx") * n_uly + lax.axis_index("uly")
    group, rank = me // size, me % size
    has_next = group < groups - 1
    has_prev = group > 0

    def device(g, r):
        flat = g * size + r
        return (flat // n_uly, flat % n_uly)

    def cols(r, width):
        return pl.ds(pl.multiple_of(r * width, width), width)

    barrier = pltpu.get_barrier_semaphore()
    for d in range(1, size):
        pl.semaphore_signal(barrier, inc=1, device_id=device(group, (rank + d) % size), device_id_type=MESH)

    @pl.when(has_next)
    def _():
        pl.semaphore_signal(barrier, inc=1, device_id=device(group + 1, rank), device_id_type=MESH)

    @pl.when(has_prev)
    def _():
        pl.semaphore_signal(barrier, inc=1, device_id=device(group - 1, rank), device_id_type=MESH)

    pl.semaphore_wait(barrier, size - 1 + jnp.where(has_next, 1, 0) + jnp.where(has_prev, 1, 0))

    def kv_copy(h, peer):
        return [
            pltpu.make_async_remote_copy(
                src_ref=src.at[:, cols(peer * kv_heads + h, HD)],
                dst_ref=dst.at[h, size + rank],
                send_sem=kv_send.at[n, h, peer],
                recv_sem=kv_recv.at[n, h, rank],
                device_id=device(group, peer),
                device_id_type=MESH,
            )
            for n, (src, dst) in enumerate(((k_ref, k_all), (v_ref, v_all)))
        ]

    def q_copy(h, peer):
        return pltpu.make_async_remote_copy(
            src_ref=q_ref.at[:, cols(peer * kv_heads + h, width)],
            dst_ref=q_all.at[h, rank],
            send_sem=q_send.at[h, peer],
            recv_sem=q_recv.at[h, rank],
            device_id=device(group, peer),
            device_id_type=MESH,
        )

    def halo_copy(h, s):
        return [
            pltpu.make_async_remote_copy(
                src_ref=buf.at[h, size + s],
                dst_ref=buf.at[h, s],
                send_sem=halo_send.at[n, h, s],
                recv_sem=halo_recv.at[n, h, s],
                device_id=device(group + 1, rank),
                device_id_type=MESH,
            )
            for n, buf in enumerate((k_all, v_all))
        ]

    def out_copy(h, i):
        return pltpu.make_async_remote_copy(
            src_ref=out_buf.at[h, i],
            dst_ref=out_ref.at[:, cols(rank * kv_heads + h, width)],
            send_sem=out_send.at[h, i],
            recv_sem=out_recv.at[h, rank],
            device_id=device(group, i),
            device_id_type=MESH,
        )

    def own_out(h):
        return pltpu.make_async_copy(
            out_buf.at[h, rank], out_ref.at[:, cols(rank * kv_heads + h, width)], own_sem.at[0, h]
        )

    def arrived(dst, sem):
        pltpu.make_async_copy(dst, dst, sem).wait()

    def kv_arrived(h, source):
        for n, buf in enumerate((k_all, v_all)):
            arrived(buf.at[h, size + source], kv_recv.at[n, h, source])

    def forward(h, source):
        @pl.when(has_next)
        def _():
            for copy in halo_copy(h, source):
                copy.start()

    for d in range(1, size):
        for copy in kv_copy(0, (rank + d) % size):
            copy.start()
    for d in range(1, size):
        q_copy(0, (rank + d) % size).start()
    own = []
    for h in range(kv_heads):
        for n, (src, dst) in enumerate(((k_ref, k_all), (v_ref, v_all))):
            own.append(pltpu.make_async_copy(
                src.at[:, cols(rank * kv_heads + h, HD)], dst.at[h, size + rank], own_sem.at[n, h]
            ))
        own.append(pltpu.make_async_copy(
            q_ref.at[:, cols(rank * kv_heads + h, width)], q_all.at[h, rank], own_sem.at[2, h]
        ))
    for copy in own:
        copy.start()

    origin = (group - 1) * size * rows

    def find_starts(i, _):
        positions = group * size * rows + i * rows + lax.broadcasted_iota(jnp.int32, (rows, HD), 0)

        def next_doc(n, carry):
            begin, found = carry
            return begin + lens_ref[n], jnp.where(begin <= positions, begin, found)

        _, found = lax.fori_loop(
            0, lens_ref.shape[0], next_doc, (jnp.int32(0), jnp.zeros((rows, HD), jnp.int32))
        )
        starts[i] = found - origin
        return 0

    lax.fori_loop(0, size, find_starts, 0)

    for copy in own:
        copy.wait()
    for d in range(size):
        source = (rank + size - d) % size
        if d:
            kv_arrived(0, source)
        forward(0, source)
        if d:
            for h in range(1, kv_heads):
                for copy in kv_copy(h, (rank + d) % size):
                    copy.start()

    def block(h, i, slot, count, first):
        keys = count * rows
        begin = starts[i] - slot * rows
        begin = jnp.concatenate([begin] * (keys // HD), axis=1)
        place = lax.broadcasted_iota(jnp.int32, (rows, keys), 1)
        allowed = place >= begin
        if first:
            allowed = allowed & (place <= lax.broadcasted_iota(jnp.int32, (rows, keys), 0))
        key = k_all[h, pl.ds(slot, count)].reshape(keys, HD)
        value = v_all[h, pl.ds(slot, count)].reshape(keys, HD)
        for j in range(share):
            query = q_all[h, i, :, j * HD:(j + 1) * HD]
            scores = lax.dot_general(
                query, key, (((1,), (1,)), ((), ())), preferred_element_type=jnp.float32
            )
            weights = jnp.where(allowed, jnp.exp2(jnp.tanh(scores * SCALE) * CAP), 0.0)
            part = sum(weights[:, c * HD:(c + 1) * HD] for c in range(keys // HD))
            product = jnp.dot(
                weights.astype(jnp.bfloat16), value, preferred_element_type=jnp.float32
            )
            if first:
                total[i, j] = part
                acc[i, j] = product
            else:
                total[i, j] += part
                acc[i, j] += product

    for h in range(kv_heads):
        last = h == kv_heads - 1

        def own_part(i, _):
            @pl.when(i != rank)
            def _():
                arrived(q_all.at[h, i], q_recv.at[h, i])
                if not last:
                    q_copy(h + 1, i).start()

            odd = lax.rem(i, 2)
            block(h, i, size + i, 1, True)

            def step(j, _):
                block(h, i, size + odd + 2 * j, 2, False)
                return 0

            lax.fori_loop(0, lax.div(i, 2), step, 0)
            return 0

        lax.fori_loop(0, size, own_part, 0)

        def halo_part(n, _):
            i = size - 1 - n
            if not last:
                @pl.when(i != rank)
                def _():
                    kv_arrived(h + 1, i)

                forward(h + 1, i)

            @pl.when(has_prev)
            def _():
                for m, buf in enumerate((k_all, v_all)):
                    arrived(buf.at[h, i], halo_recv.at[m, h, i])

            def step(j, _):
                block(h, i, i + 2 * j, 2, False)
                return 0

            @pl.when(has_prev)
            def _():
                lax.fori_loop(0, lax.div(size + 1 - i, 2), step, 0)

            @pl.when((group == 0) & (lax.rem(i, 2) == 1))
            def _():
                block(h, i, size, 1, False)

            for j in range(share):
                row_total = jnp.sum(total[i, j], axis=1, keepdims=True)
                out_buf[h, i, :, j * HD:(j + 1) * HD] = (acc[i, j] / row_total).astype(jnp.bfloat16)

            @pl.when(i != rank)
            def _():
                out_copy(h, i).start()

            @pl.when(i == rank)
            def _():
                own_out(h).start()

            return 0

        lax.fori_loop(0, size, halo_part, 0)

    for h in range(kv_heads):
        own_out(h).wait()
        for d in range(1, size):
            peer = (rank + d) % size
            for copy in kv_copy(h, peer):
                copy.wait_send()
            q_copy(h, peer).wait_send()
            out_copy(h, peer).wait_send()
            arrived(out_ref.at[:, cols(peer * kv_heads + h, width)], out_recv.at[h, peer])

    @pl.when(has_next)
    def _():
        for h in range(kv_heads):
            for s in range(size):
                for copy in halo_copy(h, s):
                    copy.wait_send()


def shards(n_ctx, n_uly, queries, key_rows, value_rows, doc_lengths):
    size = SPAN * n_uly
    rows, q_width = queries.shape
    kv_heads = key_rows.shape[1] // size // HD
    share = q_width // key_rows.shape[1]
    dma = pltpu.SemaphoreType.DMA
    return pl.pallas_call(
        functools.partial(kernel, n_ctx, n_uly),
        out_shape=jax.ShapeDtypeStruct(queries.shape, jnp.bfloat16),
        in_specs=[pl.BlockSpec(memory_space=pltpu.SMEM)] + [pl.BlockSpec(memory_space=pl.ANY)] * 3,
        out_specs=pl.BlockSpec(memory_space=pl.ANY),
        scratch_shapes=[
            pltpu.VMEM((kv_heads, size, rows, share * HD), jnp.bfloat16),
            pltpu.VMEM((kv_heads, 2 * size, rows, HD), jnp.bfloat16),
            pltpu.VMEM((kv_heads, 2 * size, rows, HD), jnp.bfloat16),
            pltpu.VMEM((kv_heads, size, rows, share * HD), jnp.bfloat16),
            pltpu.VMEM((size, rows, HD), jnp.int32),
            pltpu.VMEM((size, share, rows, HD), jnp.float32),
            pltpu.VMEM((size, share, rows, HD), jnp.float32),
            dma((3, kv_heads)),
            dma((2, kv_heads, size)),
            dma((2, kv_heads, size)),
            dma((kv_heads, size)),
            dma((kv_heads, size)),
            dma((2, kv_heads, size)),
            dma((2, kv_heads, size)),
            dma((kv_heads, size)),
            dma((kv_heads, size)),
        ],
        compiler_params=pltpu.CompilerParams(
            collective_id=0, has_side_effects=True, vmem_limit_bytes=48 * 1024 * 1024
        ),
    )(doc_lengths, queries, key_rows, value_rows)


def solution(mesh):
    placed = (P(("ctx", "uly"), None), P(("ctx", "uly"), None), P(("ctx", "uly"), None), P())
    return jax.shard_map(
        functools.partial(shards, mesh.shape["ctx"], mesh.shape["uly"]),
        mesh=mesh, in_specs=placed, out_specs=P(("ctx", "uly"), None), check_vma=False,
    )
```

time: 123 us -> 101 us (0.82)
  Pallas kernels: 118 us -> 96.8 us
    pallas_call x1, Pallas kernels: 118 us -> 96.8 us  [shards(): pl.pallas_call(functools.partial(kernel, n_ctx, n_uly), out_shape=jax.Sha...]
where the time goes in v2:
time: 101 us
  Pallas kernels  96.8 us (96%)
  local copies, waits for them, and re-layouts  4.42 us (4%)
    pallas_call x1, Pallas kernels, shards(): pl.pallas_call(functools.partial(kernel, n_ctx, n_uly), out_shape=jax.Sha...  96.8 us
    unnamed x7, local copies, waits for them, and re-layouts  4.42 us

profile of v2, /device:TPU:8, one launch (start us, length us, event | category | flops | bytes accessed | tf_op | source)
XLA Modules:
  0.0 101.2 jit_solution(12372299879585444811)
XLA Ops:
  0.0 0.0 copy-start
  0.0 1.2 %copy-done = bf16[256,2048]{1,0:T(8,128)(2,1)S(1)} copy-done((bf16[256,2048]{1,0:T(8,128)(2,1)S(1)}, bf16[256,2048]{1,0:T(8,128)(2,1)}, u32[]{:S(2)}) %copy-start) | copy-done | bytes 1048600
  1.2 0.0 copy-start.1
  1.2 1.2 %copy-done.1 = bf16[256,2048]{1,0:T(8,128)(2,1)S(1)} copy-done((bf16[256,2048]{1,0:T(8,128)(2,1)S(1)}, bf16[256,2048]{1,0:T(8,128)(2,1)}, u32[]{:S(2)}) %copy-start.1) | copy-done | bytes 1048600
  2.5 0.0 copy-start.2
  2.5 0.7 copy-done.2
  3.1 96.8 %shard_map.46 = bf16[256,4096]{1,0:T(8,128)(2,1)S(1)} custom-call(s32[8]{0:T(128)S(1)} %copy-done.2, bf16[256,4096]{1,0:T(8,128)(2,1)} %q_ref.1, bf16[256,2048]{1,0:T(8,128)(2,1)S(1)} %copy-done, bf16[256,2048]{1,0:T(8,128)(2,1)S(1)} %copy-done.1), custom_call_target="tpu_custom_call" | custom-call | tf_op jit(solution)/shard_map/pallas_call | solution.py:282
  99.9 1.3 %copy.6 = bf16[256,4096]{1,0:T(8,128)(2,1)} copy(bf16[256,4096]{1,0:T(8,128)(2,1)S(1)} %shard_map.46) | data formatting | bytes 4194304
Async XLA Ops:
  0.0 1.2 %copy-start = (bf16[256,2048]{1,0:T(8,128)(2,1)S(1)}, bf16[256,2048]{1,0:T(8,128)(2,1)}, u32[]{:S(2)}) copy-start(bf16[256,2048]{1,0:T(8,128)(2,1)} %k_ref.1) | copy-start | bytes 3145732
  1.2 1.2 %copy-start.1 = (bf16[256,2048]{1,0:T(8,128)(2,1)S(1)}, bf16[256,2048]{1,0:T(8,128)(2,1)}, u32[]{:S(2)}) copy-start(bf16[256,2048]{1,0:T(8,128)(2,1)} %v_ref.1) | copy-start | bytes 3145732
  2.5 0.7 copy-start.2

commit v3 on v2

--- a/solution.py
+++ b/solution.py
@@ -174,22 +174,22 @@
             allowed = allowed & (place <= lax.broadcasted_iota(jnp.int32, (rows, keys), 0))
         key = k_all[h, pl.ds(slot, count)].reshape(keys, HD)
         value = v_all[h, pl.ds(slot, count)].reshape(keys, HD)
+        query = jnp.concatenate([q_all[h, i, :, j * HD:(j + 1) * HD] for j in range(share)], axis=0)
+        scores = lax.dot_general(
+            query, key, (((1,), (1,)), ((), ())), preferred_element_type=jnp.float32
+        )
+        weights = jnp.exp2(jnp.tanh(scores * SCALE) * CAP)
+        weights = jnp.where(jnp.concatenate([allowed] * share, axis=0), weights, 0.0)
+        part = sum(weights[:, c * HD:(c + 1) * HD] for c in range(keys // HD))
+        product = jnp.dot(weights.astype(jnp.bfloat16), value, preferred_element_type=jnp.float32)
         for j in range(share):
-            query = q_all[h, i, :, j * HD:(j + 1) * HD]
-            scores = lax.dot_general(
-                query, key, (((1,), (1,)), ((), ())), preferred_element_type=jnp.float32
-            )
-            weights = jnp.where(allowed, jnp.exp2(jnp.tanh(scores * SCALE) * CAP), 0.0)
-            part = sum(weights[:, c * HD:(c + 1) * HD] for c in range(keys // HD))
-            product = jnp.dot(
-                weights.astype(jnp.bfloat16), value, preferred_element_type=jnp.float32
-            )
+            own_rows = slice(j * rows, (j + 1) * rows)
             if first:
-                total[i, j] = part
-                acc[i, j] = product
+                total[i, j] = part[own_rows]
+                acc[i, j] = product[own_rows]
             else:
-                total[i, j] += part
-                acc[i, j] += product
+                total[i, j] += part[own_rows]
+                acc[i, j] += product[own_rows]
 
     for h in range(kv_heads):
         last = h == kv_heads - 1

time: 101 us -> 92.8 us (0.919)
  Pallas kernels: 96.8 us -> 88.2 us
    pallas_call x1, Pallas kernels: 96.8 us -> 88.2 us  [shards(): pl.pallas_call(functools.partial(kernel, n_ctx, n_uly), out_shape=jax.Sha...]
where the time goes in v3:
time: 92.8 us; the launch traced here: 92.6 us
  Pallas kernels  88.2 us (95%)
  local copies, waits for them, and re-layouts  4.42 us (5%)
    pallas_call x1, Pallas kernels, shards(): pl.pallas_call(functools.partial(kernel, n_ctx, n_uly), out_shape=jax.Sha...  88.2 us
    unnamed x7, local copies, waits for them, and re-layouts  4.42 us

profile of v3, /device:TPU:8, one launch (start us, length us, event | category | flops | bytes accessed | tf_op | source)
XLA Modules:
  0.0 92.6 jit_solution(7726696728644336290)
XLA Ops:
  0.0 0.0 copy-start
  0.0 1.2 %copy-done = bf16[256,2048]{1,0:T(8,128)(2,1)S(1)} copy-done((bf16[256,2048]{1,0:T(8,128)(2,1)S(1)}, bf16[256,2048]{1,0:T(8,128)(2,1)}, u32[]{:S(2)}) %copy-start) | copy-done | bytes 1048600
  1.2 0.0 copy-start.1
  1.2 1.2 %copy-done.1 = bf16[256,2048]{1,0:T(8,128)(2,1)S(1)} copy-done((bf16[256,2048]{1,0:T(8,128)(2,1)S(1)}, bf16[256,2048]{1,0:T(8,128)(2,1)}, u32[]{:S(2)}) %copy-start.1) | copy-done | bytes 1048600
  2.5 0.0 copy-start.2
  2.5 0.7 copy-done.2
  3.1 88.2 %shard_map.46 = bf16[256,4096]{1,0:T(8,128)(2,1)S(1)} custom-call(s32[8]{0:T(128)S(1)} %copy-done.2, bf16[256,4096]{1,0:T(8,128)(2,1)} %q_ref.1, bf16[256,2048]{1,0:T(8,128)(2,1)S(1)} %copy-done, bf16[256,2048]{1,0:T(8,128)(2,1)S(1)} %copy-done.1), custom_call_target="tpu_custom_call" | custom-call | tf_op jit(solution)/shard_map/pallas_call | solution.py:282
  91.3 1.3 %copy.6 = bf16[256,4096]{1,0:T(8,128)(2,1)} copy(bf16[256,4096]{1,0:T(8,128)(2,1)S(1)} %shard_map.46) | data formatting | bytes 4194304
Async XLA Ops:
  0.0 1.2 %copy-start = (bf16[256,2048]{1,0:T(8,128)(2,1)S(1)}, bf16[256,2048]{1,0:T(8,128)(2,1)}, u32[]{:S(2)}) copy-start(bf16[256,2048]{1,0:T(8,128)(2,1)} %k_ref.1) | copy-start | bytes 3145732
  1.2 1.2 %copy-start.1 = (bf16[256,2048]{1,0:T(8,128)(2,1)S(1)}, bf16[256,2048]{1,0:T(8,128)(2,1)}, u32[]{:S(2)}) copy-start(bf16[256,2048]{1,0:T(8,128)(2,1)} %v_ref.1) | copy-start | bytes 3145732
  2.5 0.7 copy-start.2

commit v4 on v3

--- a/solution.py
+++ b/solution.py
@@ -123,6 +123,10 @@
             copy.start()
     for d in range(1, size):
         q_copy(0, (rank + d) % size).start()
+    for h in range(1, kv_heads):
+        for d in range(1, size):
+            for copy in kv_copy(h, (rank + d) % size):
+                copy.start()
     own = []
     for h in range(kv_heads):
         for n, (src, dst) in enumerate(((k_ref, k_all), (v_ref, v_all))):
@@ -159,10 +163,6 @@
         if d:
             kv_arrived(0, source)
         forward(0, source)
-        if d:
-            for h in range(1, kv_heads):
-                for copy in kv_copy(h, (rank + d) % size):
-                    copy.start()
 
     def block(h, i, slot, count, first):
         keys = count * rows

time: 92.8 us -> 92.8 us (level)
  no operation moved by 1% of the time
where the time goes in v4:
time: 92.8 us; the launch traced here: 92.6 us
  Pallas kernels  88.2 us (95%)
  local copies, waits for them, and re-layouts  4.42 us (5%)
    pallas_call x1, Pallas kernels, shards(): pl.pallas_call(functools.partial(kernel, n_ctx, n_uly), out_shape=jax.Sha...  88.2 us
    unnamed x7, local copies, waits for them, and re-layouts  4.42 us

profile of v4, /device:TPU:8, one launch (start us, length us, event | category | flops | bytes accessed | tf_op | source)
XLA Modules:
  0.0 92.6 jit_solution(16063249875147054415)
XLA Ops:
  0.0 0.0 copy-start
  0.0 1.2 %copy-done = bf16[256,2048]{1,0:T(8,128)(2,1)S(1)} copy-done((bf16[256,2048]{1,0:T(8,128)(2,1)S(1)}, bf16[256,2048]{1,0:T(8,128)(2,1)}, u32[]{:S(2)}) %copy-start) | copy-done | bytes 1048600
  1.2 0.0 copy-start.1
  1.2 1.2 %copy-done.1 = bf16[256,2048]{1,0:T(8,128)(2,1)S(1)} copy-done((bf16[256,2048]{1,0:T(8,128)(2,1)S(1)}, bf16[256,2048]{1,0:T(8,128)(2,1)}, u32[]{:S(2)}) %copy-start.1) | copy-done | bytes 1048600
  2.5 0.0 copy-start.2
  2.5 0.7 copy-done.2
  3.1 88.2 %shard_map.46 = bf16[256,4096]{1,0:T(8,128)(2,1)S(1)} custom-call(s32[8]{0:T(128)S(1)} %copy-done.2, bf16[256,4096]{1,0:T(8,128)(2,1)} %q_ref.1, bf16[256,2048]{1,0:T(8,128)(2,1)S(1)} %copy-done, bf16[256,2048]{1,0:T(8,128)(2,1)S(1)} %copy-done.1), custom_call_target="tpu_custom_call" | custom-call | tf_op jit(solution)/shard_map/pallas_call | solution.py:282
  91.3 1.3 %copy.6 = bf16[256,4096]{1,0:T(8,128)(2,1)} copy(bf16[256,4096]{1,0:T(8,128)(2,1)S(1)} %shard_map.46) | data formatting | bytes 4194304
Async XLA Ops:
  0.0 1.2 %copy-start = (bf16[256,2048]{1,0:T(8,128)(2,1)S(1)}, bf16[256,2048]{1,0:T(8,128)(2,1)}, u32[]{:S(2)}) copy-start(bf16[256,2048]{1,0:T(8,128)(2,1)} %k_ref.1) | copy-start | bytes 3145732
  1.2 1.2 %copy-start.1 = (bf16[256,2048]{1,0:T(8,128)(2,1)S(1)}, bf16[256,2048]{1,0:T(8,128)(2,1)}, u32[]{:S(2)}) copy-start(bf16[256,2048]{1,0:T(8,128)(2,1)} %v_ref.1) | copy-start | bytes 3145732
  2.5 0.7 copy-start.2
